TPU v7x, 32 devices: a whole 2x2x4 slice. The times are simulated.
32 devices in a mesh: groups: 2 (over x), zero: 16 (over z, y, core).
Axes of the slice: x: 2, y: 2, z: 4, core: 2. Of those that a mesh axis runs over, the one named last changes fastest.
Arguments:
- features: bfloat16 [8192, 8192], P(('groups', 'zero')), parts along dimension 0, may hold values from -6 to 6
- grad_out: bfloat16 [8192, 1024], P(('groups', 'zero')), parts along dimension 0, may hold values from -6 to 6
- base_weight: bfloat16 [8192, 1024], P('zero'), may hold values from -0.0625 to 0.0625
- factor_a: bfloat16 [16, 8192, 16], P('zero'), may hold values from -0.0625 to 0.0625
- factor_b: bfloat16 [16, 16, 1024], P('zero'), may hold values from -0.1875 to 0.1875
- tenant_ids: int32 [8192], P(('groups', 'zero')), parts along dimension 0, may hold values from 0 to 15, as said below
- owner_of: int32 [16], replicated, may hold values from 0 to 15, as said below
Outputs:
- grad_in: bfloat16 [8192, 8192], P(('groups', 'zero')), parts along dimension 0
- grad_a: float32 [32, 8192, 16], P(('groups', 'zero')), parts along dimension 0
- grad_b: float32 [32, 16, 1024], P(('groups', 'zero')), parts along dimension 0
There are 2 independent parts, one for each index of `groups`. A program takes and returns all parts, laid end to end along the dimension named above; an argument that names none is the same for every part. Nothing has to cross between parts.
Inputs may be any that keep to these rules, and one draw needn't show every extreme that they name: `tenant_ids`: ids are constant on aligned blocks of 128 rows, never fall along the rows of a group, and every tenant has at least one block. `owner_of`: every device index owns the same number of tenants, 1.
All inputs are finite; a program needn't handle non-finite values.
Results may differ from a plain program's by a relative error of at most 0.0034.
Values may be sent and summed in bfloat16 or wider, within the bound.
A program may use at most 128 MiB of HBM per device.

v0:
```python
import jax
import jax.numpy as jnp
from jax import lax
from jax.sharding import PartitionSpec as P

BLK = 128
TEN_DEV = 1


low_rank_scale = 2.0


def slot_table(owner_of):
    tenant_count = owner_of.shape[0]
    positions = jnp.arange(tenant_count, dtype=jnp.int32)
    before = (owner_of[None, :] == owner_of[:, None]) & (positions[None, :] < positions[:, None])
    return owner_of * TEN_DEV + jnp.sum(before.astype(jnp.int32), axis=1)


def body(features, grad_out, base_weight, factor_a, factor_b, tenant_ids, owner_of):
    width_zero = lax.axis_size("zero")
    row_count = features.shape[0]
    model_width = features.shape[1]
    kv_width = grad_out.shape[1]
    rank_width = factor_a.shape[2]
    tenant_count = owner_of.shape[0]
    block_count = row_count // BLK
    piece_a = model_width * rank_width // width_zero
    piece_b = rank_width * kv_width // width_zero
    block_ids = tenant_ids.reshape(block_count, BLK)[:, 0]
    every_id = lax.all_gather(block_ids, "zero", axis=0, tiled=True)
    slots = slot_table(owner_of)
    every_slot = jnp.take(slots, every_id)
    targets = jnp.arange(tenant_count, dtype=jnp.int32)
    member = (every_slot[None, :] == targets[:, None]).astype(jnp.float32)
    counts = BLK * jnp.sum(member, axis=1)
    shares = member / counts[:, None]
    flat_a = factor_a.reshape(TEN_DEV, width_zero, piece_a)
    flat_b = factor_b.reshape(TEN_DEV, width_zero, piece_b)
    held_a, held_b = (
        lax.all_to_all(flat_a, "zero", split_axis=1, concat_axis=0, tiled=True),
        lax.all_to_all(flat_b, "zero", split_axis=1, concat_axis=0, tiled=True),
    )
    wanted_a = jnp.take(held_a.reshape(tenant_count, piece_a), every_slot, axis=0).reshape(
        width_zero, block_count, piece_a
    )
    wanted_b = jnp.take(held_b.reshape(tenant_count, piece_b), every_slot, axis=0).reshape(
        width_zero, block_count, piece_b
    )
    got_a, got_b = (
        lax.all_to_all(wanted_a, "zero", split_axis=0, concat_axis=2, tiled=True),
        lax.all_to_all(wanted_b, "zero", split_axis=0, concat_axis=2, tiled=True),
    )
    a_blocks = got_a.reshape(block_count, model_width, rank_width)
    b_blocks = got_b.reshape(block_count, rank_width, kv_width)
    blocked_in = features.reshape(block_count, BLK, model_width)
    blocked_out = grad_out.reshape(block_count, BLK, kv_width)
    low_proj = (
        low_rank_scale
        * jnp.einsum("nrk,njk->nrj", blocked_out, b_blocks, preferred_element_type=jnp.float32)
    ).astype(jnp.bfloat16)
    correction = jnp.einsum(
        "nrj,ndj->nrd", low_proj, a_blocks, preferred_element_type=jnp.float32
    ).reshape(row_count, model_width)
    inner = jnp.einsum(
        "nrd,ndj->nrj", blocked_in, a_blocks, preferred_element_type=jnp.float32
    ).astype(jnp.bfloat16)
    part_a = jnp.einsum("nrd,nrj->ndj", blocked_in, low_proj, preferred_element_type=jnp.float32)
    part_b = low_rank_scale * jnp.einsum(
        "nrj,nrk->njk", inner, blocked_out, preferred_element_type=jnp.float32
    )
    full_weight = lax.all_gather(base_weight, "zero", axis=0, tiled=True)
    base = lax.dot_general(
        grad_out, full_weight, (((1,), (1,)), ((), ())), preferred_element_type=jnp.float32
    )
    grad_in = (base + correction).astype(jnp.bfloat16)
    sent_a, sent_b = (
        lax.all_to_all(
            part_a.reshape(block_count, width_zero, piece_a),
            "zero",
            split_axis=1,
            concat_axis=0,
            tiled=True,
        ),
        lax.all_to_all(
            part_b.reshape(block_count, width_zero, piece_b),
            "zero",
            split_axis=1,
            concat_axis=0,
            tiled=True,
        ),
    )
    summed_a = jnp.dot(
        shares, sent_a.reshape(width_zero * block_count, piece_a), precision=lax.Precision.HIGHEST
    )
    summed_b = jnp.dot(
        shares, sent_b.reshape(width_zero * block_count, piece_b), precision=lax.Precision.HIGHEST
    )
    owned_a, owned_b = (
        lax.all_to_all(summed_a, "zero", split_axis=0, concat_axis=1, tiled=True),
        lax.all_to_all(summed_b, "zero", split_axis=0, concat_axis=1, tiled=True),
    )
    grad_b = owned_b.reshape(TEN_DEV, rank_width, kv_width)
    grad_a = owned_a.reshape(TEN_DEV, model_width, rank_width)
    return (grad_in, grad_a, grad_b)


def solution(mesh):
    placed = (
        P(("groups", "zero"), None),
        P(("groups", "zero"), None),
        P("zero", None),
        P("zero", None, None),
        P("zero", None, None),
        P(("groups", "zero")),
        P(),
    )
    return jax.shard_map(
        body,
        mesh=mesh,
        in_specs=placed,
        out_specs=(
            P(("groups", "zero"), None),
            P(("groups", "zero"), None, None),
            P(("groups", "zero"), None, None),
        ),
        check_vma=False,
    )
```

profile of v0, /device:TPU:0, one launch (start us, length us, event | category | flops | bytes accessed | tf_op | source)
XLA Modules:
  0.0 231.9 jit_solution(15251654851346844919)
XLA Ops:
  7.2 0.0 copy-start
  7.2 0.0 all-gather.3.cloned.1.call-start
  7.2 0.7 all-gather.3.cloned.1.call-update
  7.9 0.8 copy.89
  8.7 0.5 broadcast.64
  9.2 0.8 reduce.3
  10.1 0.6 reshape.161
  10.7 7.4 %all-to-all-start = ((bf16[16,2,512]{2,1,0:T(2,128)(2,1)}), bf16[16,2,512]{2,1,0:T(2,128)(2,1)S(1)}, u32[]{:S(2)}, u32[]{:S(2)}) async-start(bf16[16,2,512]{2,1,0:T(2,128)(2,1)} %reshape.161), calls=%async_computation | async-start | bytes 65536 | tf_op jit(solution)/shard_map/all_to_all | solution.py:42
  18.1 0.9 convert_reduce_fusion.1
  19.0 0.7 add.30
  19.7 1.2 dynamic-slice
  21.6 0.8 slice_reduce_fusion
  22.4 0.2 dynamic-update-slice
  22.6 12.5 %all-reduce = s32[32]{0:T(128)S(1)} all-reduce(s32[32]{0:T(128)S(1)} %dynamic-update-slice), channel_id=2, replica_groups=mesh['groups'=2,'zero'=16] {'zero'}, use_global_device_ids=true, to_apply=%add | all-reduce | flops 32 | bytes 256 | tf_op jit(solution)/shard_map/all_gather | solution.py:31
  35.2 0.7 gather_fusion
  35.9 0.1 broadcast_in_dim.39
  36.0 1.9 copy.64
  37.9 1.5 reshape.158
  39.3 2.2 reduce.4
  41.5 0.9 reshape.163
  42.4 0.0 all-to-all-done
  42.4 3.5 %all-to-all-start.2 = ((bf16[16,2,4096]{2,1,0:T(2,128)(2,1)}), bf16[16,2,4096]{2,1,0:T(2,128)(2,1)S(1)}, u32[]{:S(2)}, u32[]{:S(2)}) async-start(bf16[16,2,4096]{2,1,0:T(2,128)(2,1)} %reshape.163), calls=%async_computation.2 | async-start | bytes 524288 | tf_op jit(solution)/shard_map/all_to_all | solution.py:41
  46.0 0.6 gather_fusion.1
  46.7 0.8 broadcast_select_fusion.1
  47.5 13.0 %all-to-all-done.2 = bf16[16,2,4096]{2,1,0:T(2,128)(2,1)S(1)} async-done(((bf16[16,2,4096]{2,1,0:T(2,128)(2,1)}), bf16[16,2,4096]{2,1,0:T(2,128)(2,1)S(1)}, u32[]{:S(2)}, u32[]{:S(2)}) %all-to-all-start.2) | async-done | bytes 262176 | tf_op jit(solution)/shard_map/all_to_all | solution.py:41
  60.5 5.6 %all-to-all-start.1 = ((bf16[16,2,1024]{2,1,0:T(2,128)(2,1)}), bf16[16,2,1024]{2,1,0:T(2,128)(2,1)S(1)}, u32[]{:S(2)}, u32[]{:S(2)}) async-start(bf16[16,2,1024]{2,1,0:T(2,128)(2,1)} %broadcast_select_fusion.1), calls=%async_computation.1 | async-start | bytes 131072 | tf_op jit(solution)/shard_map/all_to_all | solution.py:52
  66.1 0.3 reshape.164
  66.4 0.3 copy.87
  66.7 0.9 gather_fusion.2
  67.6 0.3 gather.20
  67.9 1.3 broadcast_select_fusion
  69.2 3.8 %all-to-all-done.1 = bf16[16,2,1024]{2,1,0:T(2,128)(2,1)S(1)} async-done(((bf16[16,2,1024]{2,1,0:T(2,128)(2,1)}), bf16[16,2,1024]{2,1,0:T(2,128)(2,1)S(1)}, u32[]{:S(2)}, u32[]{:S(2)}) %all-to-all-start.1) | async-done | bytes 65568 | tf_op jit(solution)/shard_map/all_to_all | solution.py:52
  73.0 3.6 %all-to-all-start.3 = ((bf16[16,2,8192]{2,1,0:T(2,128)(2,1)}), bf16[16,2,8192]{2,1,0:T(2,128)(2,1)S(1)}, u32[]{:S(2)}, u32[]{:S(2)}) async-start(bf16[16,2,8192]{2,1,0:T(2,128)(2,1)} %broadcast_select_fusion), calls=%async_computation.3 | async-start | bytes 1048576 | tf_op jit(solution)/shard_map/all_to_all | solution.py:51
  76.6 0.2 fusion.1
  76.8 22.8 %all-to-all-done.3 = bf16[16,2,8192]{2,1,0:T(2,128)(2,1)S(1)} async-done(((bf16[16,2,8192]{2,1,0:T(2,128)(2,1)}), bf16[16,2,8192]{2,1,0:T(2,128)(2,1)S(1)}, u32[]{:S(2)}, u32[]{:S(2)}) %all-to-all-start.3) | async-done | bytes 524320 | tf_op jit(solution)/shard_map/all_to_all | solution.py:51
  99.6 0.3 copy.66
  99.9 4.5 %reshape.116 = bf16[2,8192,16]{2,1,0:T(8,128)(2,1)} reshape(bf16[1,2,16,8192]{3,2,1,0:T(8,128)(2,1)S(1)} %copy.66) | data formatting | bytes 1048576 | tf_op jit(solution)/shard_map/reshape | solution.py:54
  104.4 5.3 %convolution_multiply_fusion = f32[2,16,1024]{2,1,0:T(8,128)S(1)} fusion(bf16[2,128,1024]{2,1,0:T(8,128)(2,1)S(1)} %bitcast.59, bf16[2,8192,16]{2,1,0:T(8,128)(2,1)} %reshape.116, bf16[2,128,8192]{2,1,0:T(8,128)(2,1)} %bitcast.62), kind=kOutput, calls=%fused_computation.7 | convolution fusion | flops 75534336 | bytes 5373952 | tf_op jit(solution)/shard_map/nrj,nrk->njk/dot_general | solution.py:69
  109.6 0.8 copy.72
  110.4 10.3 %all-to-all-start.6 = ((f32[2,16,1024]{2,0,1:T(2,128)}), f32[2,16,1024]{2,0,1:T(2,128)S(1)}, u32[]{:S(2)}, u32[]{:S(2)}) async-start(f32[2,16,1024]{2,0,1:T(2,128)} %copy.72), calls=%async_computation.6 | async-start | bytes 262144 | tf_op jit(solution)/shard_map/all_to_all | solution.py:85
  120.7 2.8 %convolution_bitcast_fusion = f32[2,8192,16]{1,2,0:T(8,128)S(1)} fusion(bf16[2,16,128]{2,1,0:T(8,128)(2,1)S(1)} %fusion.1, bf16[2,128,8192]{2,1,0:T(8,128)(2,1)} %bitcast.63), kind=kOutput, calls=%fused_computation.5 | convolution fusion | flops 67108864 | bytes 5251072 | tf_op jit(solution)/shard_map/nrd,nrj->ndj/dot_general | solution.py:68
  123.5 4.6 %copy.68 = f32[2,8192,16]{2,1,0:T(8,128)} copy(f32[2,8192,16]{1,2,0:T(8,128)S(1)} %convolution_bitcast_fusion) | data formatting | bytes 2097152 | tf_op jit(solution)/shard_map/nrd,nrj->ndj/dot_general | solution.py:68
  128.2 7.9 %reshape.119 = f32[2,16,8192]{2,1,0:T(8,128)S(1)} reshape(f32[2,8192,16]{2,1,0:T(8,128)} %copy.68) | data formatting | bytes 2097152 | tf_op jit(solution)/shard_map/reshape | solution.py:79
  136.0 1.8 copy.69
  137.8 0.0 all-to-all-done.6
  137.8 6.3 %all-to-all-start.4 = ((f32[2,16,8192]{2,0,1:T(2,128)}), f32[2,16,8192]{2,0,1:T(2,128)S(1)}, u32[]{:S(2)}, u32[]{:S(2)}) async-start(f32[2,16,8192]{2,0,1:T(2,128)} %copy.69), calls=%async_computation.4 | async-start | bytes 2097152 | tf_op jit(solution)/shard_map/all_to_all | solution.py:78
  144.1 0.1 convert_reduce_fusion
  144.3 0.1 reshape.122
  144.4 0.3 convolution_bitcast_fusion.2
  144.6 0.7 copy.73
  145.3 28.3 %all-to-all-done.4 = f32[2,16,8192]{2,0,1:T(2,128)S(1)} async-done(((f32[2,16,8192]{2,0,1:T(2,128)}), f32[2,16,8192]{2,0,1:T(2,128)S(1)}, u32[]{:S(2)}, u32[]{:S(2)}) %all-to-all-start.4) | async-done | bytes 1048608 | tf_op jit(solution)/shard_map/all_to_all | solution.py:78
  173.7 6.6 %all-to-all-start.7 = ((f32[16,1,1024]{2,1,0:T(1,128)}), f32[16,1,1024]{2,1,0:T(1,128)S(1)}, u32[]{:S(2)}, u32[]{:S(2)}) async-start(f32[16,1,1024]{2,1,0:T(1,128)} %copy.73), calls=%async_computation.7 | async-start | bytes 131072 | tf_op jit(solution)/shard_map/all_to_all | solution.py:101
  180.2 0.7 reshape.120
  181.0 0.6 convolution_bitcast_fusion.1
  181.6 1.3 copy.70
  183.0 4.2 %all-to-all-done.7 = f32[16,1,1024]{2,1,0:T(1,128)S(1)} async-done(((f32[16,1,1024]{2,1,0:T(1,128)}), f32[16,1,1024]{2,1,0:T(1,128)S(1)}, u32[]{:S(2)}, u32[]{:S(2)}) %all-to-all-start.7) | async-done | bytes 65568 | tf_op jit(solution)/shard_map/all_to_all | solution.py:101
  187.1 3.8 %all-to-all-start.5 = ((f32[16,1,8192]{2,1,0:T(1,128)}), f32[16,1,8192]{2,1,0:T(1,128)S(1)}, u32[]{:S(2)}, u32[]{:S(2)}) async-start(f32[16,1,8192]{2,1,0:T(1,128)} %copy.70), calls=%async_computation.5 | async-start | bytes 1048576 | tf_op jit(solution)/shard_map/all_to_all | solution.py:100
  190.9 6.7 %fusion.9 = f32[2,128,8192]{2,1,0:T(8,128)} fusion(bf16[2,16,128]{2,1,0:T(8,128)(2,1)S(1)} %fusion.1, bf16[2,8192,16]{2,1,0:T(8,128)(2,1)} %reshape.116), kind=kOutput, calls=%fused_computation.37 | convolution fusion | flops 67108864 | bytes 8921088 | tf_op jit(solution)/shard_map/nrj,ndj->nrd/dot_general | solution.py:62
  197.6 0.6 copy.75
  198.3 6.9 %all-to-all-done.5 = f32[16,1,8192]{2,1,0:T(1,128)S(1)} async-done(((f32[16,1,8192]{2,1,0:T(1,128)}), f32[16,1,8192]{2,1,0:T(1,128)S(1)}, u32[]{:S(2)}, u32[]{:S(2)}) %all-to-all-start.5) | async-done | bytes 524320 | tf_op jit(solution)/shard_map/all_to_all | solution.py:100
  205.1 1.2 reduce.1
  206.4 2.8 %reshape.121 = f32[1,8192,16]{2,1,0:T(8,128)} reshape(f32[16,8192]{1,0:T(8,128)S(1)} %reduce.1) | data formatting | bytes 1048576 | tf_op jit(solution)/shard_map/reshape | solution.py:104
  209.2 3.5 %copy.74 = f32[1,8192,16]{1,2,0:T(8,128)} copy(f32[1,8192,16]{2,1,0:T(8,128)} %reshape.121) | data formatting | bytes 1048576
  212.7 12.3 %fusion = bf16[256,8192]{1,0:T(8,128)(2,1)} fusion(f32[256,8192]{1,0:T(8,128)} %bitcast.61, bf16[256,1024]{1,0:T(8,128)(2,1)S(1)} %copy-done, bf16[8192,1024]{1,0:T(8,128)(2,1)} %all-gather.3.cloned.1.call-done), kind=kOutput, calls=%fused_computation.4 | convolution fusion | flops 4299161600 | bytes 29884416 | tf_op jit(solution)/shard_map/dot_general | solution.py:73
  (12 shorter events, 0.1 us)
Async XLA Ops:
  7.2 69.4 %copy-start = (bf16[256,1024]{1,0:T(8,128)(2,1)S(1)}, bf16[256,1024]{1,0:T(8,128)(2,1)}, u32[]{:S(2)}) copy-start(bf16[256,1024]{1,0:T(8,128)(2,1)} %param.8) | copy-start | bytes 1572868
  7.2 205.5 %all-gather.3.cloned.1.call-start = ((), (), s32[]{:S(2)}) async-start(), calls=%async_computation.8 | async-start | bytes 17825792 | tf_op jit(solution)/shard_map/all_gather | solution.py:72
  10.7 31.7 %all-to-all-start = ((bf16[16,2,512]{2,1,0:T(2,128)(2,1)}), bf16[16,2,512]{2,1,0:T(2,128)(2,1)S(1)}, u32[]{:S(2)}, u32[]{:S(2)}) async-start(bf16[16,2,512]{2,1,0:T(2,128)(2,1)} %reshape.161), calls=%async_computation | async-start | bytes 65536 | tf_op jit(solution)/shard_map/all_to_all | solution.py:42
  42.4 18.1 %all-to-all-start.2 = ((bf16[16,2,4096]{2,1,0:T(2,128)(2,1)}), bf16[16,2,4096]{2,1,0:T(2,128)(2,1)S(1)}, u32[]{:S(2)}, u32[]{:S(2)}) async-start(bf16[16,2,4096]{2,1,0:T(2,128)(2,1)} %reshape.163), calls=%async_computation.2 | async-start | bytes 524288 | tf_op jit(solution)/shard_map/all_to_all | solution.py:41
  60.5 12.5 %all-to-all-start.1 = ((bf16[16,2,1024]{2,1,0:T(2,128)(2,1)}), bf16[16,2,1024]{2,1,0:T(2,128)(2,1)S(1)}, u32[]{:S(2)}, u32[]{:S(2)}) async-start(bf16[16,2,1024]{2,1,0:T(2,128)(2,1)} %broadcast_select_fusion.1), calls=%async_computation.1 | async-start | bytes 131072 | tf_op jit(solution)/shard_map/all_to_all | solution.py:52
  73.0 26.6 %all-to-all-start.3 = ((bf16[16,2,8192]{2,1,0:T(2,128)(2,1)}), bf16[16,2,8192]{2,1,0:T(2,128)(2,1)S(1)}, u32[]{:S(2)}, u32[]{:S(2)}) async-start(bf16[16,2,8192]{2,1,0:T(2,128)(2,1)} %broadcast_select_fusion), calls=%async_computation.3 | async-start | bytes 1048576 | tf_op jit(solution)/shard_map/all_to_all | solution.py:51
  110.4 27.4 %all-to-all-start.6 = ((f32[2,16,1024]{2,0,1:T(2,128)}), f32[2,16,1024]{2,0,1:T(2,128)S(1)}, u32[]{:S(2)}, u32[]{:S(2)}) async-start(f32[2,16,1024]{2,0,1:T(2,128)} %copy.72), calls=%async_computation.6 | async-start | bytes 262144 | tf_op jit(solution)/shard_map/all_to_all | solution.py:85
  137.8 35.8 %all-to-all-start.4 = ((f32[2,16,8192]{2,0,1:T(2,128)}), f32[2,16,8192]{2,0,1:T(2,128)S(1)}, u32[]{:S(2)}, u32[]{:S(2)}) async-start(f32[2,16,8192]{2,0,1:T(2,128)} %copy.69), calls=%async_computation.4 | async-start | bytes 2097152 | tf_op jit(solution)/shard_map/all_to_all | solution.py:78
  173.7 13.5 %all-to-all-start.7 = ((f32[16,1,1024]{2,1,0:T(1,128)}), f32[16,1,1024]{2,1,0:T(1,128)S(1)}, u32[]{:S(2)}, u32[]{:S(2)}) async-start(f32[16,1,1024]{2,1,0:T(1,128)} %copy.73), calls=%async_computation.7 | async-start | bytes 131072 | tf_op jit(solution)/shard_map/all_to_all | solution.py:101
  187.1 18.0 %all-to-all-start.5 = ((f32[16,1,8192]{2,1,0:T(1,128)}), f32[16,1,8192]{2,1,0:T(1,128)S(1)}, u32[]{:S(2)}, u32[]{:S(2)}) async-start(f32[16,1,8192]{2,1,0:T(1,128)} %copy.70), calls=%async_computation.5 | async-start | bytes 1048576 | tf_op jit(solution)/shard_map/all_to_all | solution.py:100
Sparse Core Ops, SparseCore 0:
  10.2 163.3 all-gather.2
where the time goes:
time: 233 us; the launch traced here: 232 us
  waiting for transfers between devices  79.6 us (34%)
  starting transfers between devices  47.1 us (20%)
  local copies, waits for them, and re-layouts  41.3 us (18%)
  matrix products  28.3 us (12%)
  between operations  14.9 us (6%)
  blocking collectives  12.5 us (5%)
  other arithmetic  8.06 us (3%)
    all_to_all x1, waiting for transfers between devices, body(): lax.all_to_all(part_a.reshape(block_count, width_zero, piece_a), 'zero',...  28.3 us
    all_to_all x1, waiting for transfers between devices, body(): lax.all_to_all(wanted_a, 'zero', split_axis=0, concat_axis=2, tiled=True)  22.8 us
    all_to_all x1, waiting for transfers between devices, body(): lax.all_to_all(flat_a, 'zero', split_axis=1, concat_axis=0, tiled=True)  13 us
    all_gather x1, blocking collectives, body(): every_id = lax.all_gather(block_ids, 'zero', axis=0, tiled=True)  12.5 us
    dot_general x1, matrix products, body(): lax.dot_general(grad_out, full_weight, (((1,), (1,)), ((), ())), preferre...  12.3 us
    unnamed x16, local copies, waits for them, and re-layouts  11 us
    all_to_all x1, starting transfers between devices, body(): lax.all_to_all(part_b.reshape(block_count, width_zero, piece_b), 'zero',...  10.3 us
    reshape x2, local copies, waits for them, and re-layouts, body(): part_a.reshape(block_count, width_zero, piece_a)  9.67 us
  transfers between devices with their start and end apart: 9, of which 6 were waited for; matrix products, arithmetic and copies ran while one was open for 28% of the time, Pallas kernels for 0%

commit v1 on v0

v1 whole, which is shorter than its diff:
```python
import functools

import jax
import jax.numpy as jnp
from jax import lax
from jax.experimental import pallas as pl
from jax.experimental.pallas import tpu as pltpu
from jax.sharding import PartitionSpec as P

BLK = 128
LANES = 128
low_rank_scale = 2.0
MESH = pl.DeviceIdType.MESH
NT = (((1,), (1,)), ((), ()))
TN = (((0,), (0,)), ((), ()))
CW, CCW, ACROSS, SIB_CW, SIB_CCW, SIB_ACROSS, SIB_OWN = range(7)


def slot_table(owner_of):
    tenant_count = owner_of.shape[0]
    positions = jnp.arange(tenant_count, dtype=jnp.int32)
    before = (owner_of[None, :] == owner_of[:, None]) & (positions[None, :] < positions[:, None])
    return owner_of + jnp.sum(before.astype(jnp.int32), axis=1)


def chip_at(pos, chips):
    if chips == 8:
        return 2 * pos + (pos // 4) * (15 - 4 * pos)
    return pos


def pos_of(chip, chips):
    if chips == 8:
        z, y = chip // 2, chip % 2
        return z + y * (7 - 2 * z)
    return chip


class Gather:
    def __init__(self, where, region, send, recv):
        self.where, self.region, self.send, self.recv = where, region, send, recv
        self.started, self.received = [], set()

    def copy(self, kind, s):
        g, across, r, core, me, sib, n = self.where
        if kind == SIB_OWN:
            pos, part = r, None
        elif kind == CW:
            pos, part = r - s + n, 0
        elif kind == CCW:
            pos, part = r + s, 1
        elif kind in (ACROSS, SIB_CW):
            pos, part = r - 1 - s + n, 0
        elif kind == SIB_CCW:
            pos, part = r + 1 + s, 1
        else:
            pos, part = r - 1 - s + n, 2
        if kind == CW:
            to = (g, chip_at((r + 1) % n, n) * 2 + core)
        elif kind == CCW:
            to = (g, chip_at((r + n - 1) % n, n) * 2 + core)
        elif kind == ACROSS:
            to = (across, me)
        else:
            to = (g, sib)
        ref = self.region(chip_at(pos % n, n) * 2 + core, part)
        return pltpu.make_async_remote_copy(
            src_ref=ref,
            dst_ref=ref,
            send_sem=self.send.at[kind, s],
            recv_sem=self.recv.at[kind, s],
            device_id=to,
            device_id_type=MESH,
        )

    def start(self, kind, s):
        self.copy(kind, s).start()
        self.started.append((kind, s))

    def need(self, kind, s):
        if (kind, s) not in self.received:
            self.received.add((kind, s))
            self.copy(kind, s).wait_recv()

    def begin(self):
        self.start(CW, 0)
        self.start(CCW, 0)
        self.start(SIB_OWN, 0)

    def step(self, s):
        n = self.where[-1]
        self.need(CW, s)
        if s < n - 2:
            self.start(CW, s + 1)
        self.start(ACROSS, s)
        self.start(SIB_CW, s)
        self.need(CCW, s)
        if s < n - 2:
            self.start(CCW, s + 1)
        self.start(SIB_CCW, s)
        if s >= 1:
            self.need(ACROSS, s - 1)
            self.start(SIB_ACROSS, s - 1)
        if s == n - 2:
            self.need(ACROSS, s)
            self.start(SIB_ACROSS, s)

    def whole(self, d):
        n = self.where[-1]
        if d == 0:
            self.need(SIB_OWN, 0)
        else:
            for own, other, s in (
                (CW, SIB_CW, d - 1),
                (CCW, SIB_CCW, n - 1 - d),
                (ACROSS, SIB_ACROSS, d - 1),
            ):
                self.need(own, s)
                self.need(other, s)

    def end(self):
        for kind, s in self.started:
            self.copy(kind, s).wait_send()


def kernel(
    zero, slots, feat_in, go, w_in, at_in, b_in, gi, ga, gb,
    feat, out, wg, abg, a_sel, low, sent, got, summed, final,
    load, stored, w_send, w_recv, ab_send, ab_recv, p_send, p_recv, f_send, f_recv,
):
    g, me = lax.axis_index("groups"), lax.axis_index("zero")
    n = zero // 2
    core = me % 2
    sib = me + 1 - 2 * core
    parity = g % 2
    across = g + 1 - 2 * parity
    r = pos_of(me // 2, n)
    rows, width = feat.shape
    blocks = rows // BLK
    rank = at_in.shape[0]
    kv = b_in.shape[1]
    held = w_in.shape[0]
    picked = blocks * rank
    piece = width // zero
    tenants = zero

    loads = [
        pltpu.make_async_copy(at_in, abg.at[me, :, pl.ds(0, width)], load.at[0]),
        pltpu.make_async_copy(b_in, abg.at[me, :, pl.ds(width, kv)], load.at[1]),
        pltpu.make_async_copy(w_in, wg.at[me], load.at[2]),
        pltpu.make_async_copy(feat_in, feat, load.at[3]),
    ]
    for copy in loads:
        copy.start()

    barrier = pltpu.get_barrier_semaphore()
    pl.semaphore_signal(barrier, inc=1, device_id=(across, me), device_id_type=MESH)

    def greet(i, c):
        pl.semaphore_signal(
            barrier, inc=1, device_id=(g, (me + i) % zero), device_id_type=MESH
        )
        return c

    lax.fori_loop(1, zero, greet, 0)
    pl.semaphore_wait(barrier, zero)

    w_third = -(-held // 48) * 16
    ab_third = -(-(width + kv) // (3 * LANES)) * LANES

    def cut(total, third, part, unit):
        if part == 1:
            return pl.ds(third, total - 2 * third)
        at = (parity if part == 0 else 1 - parity) * (total - third)
        return pl.ds(pl.multiple_of(at, unit), third)

    def w_region(i, part):
        return wg.at[i] if part is None else wg.at[i, cut(held, w_third, part, 16), :]

    def ab_region(i, part):
        if part is None:
            return abg.at[i]
        return abg.at[i, :, cut(width + kv, ab_third, part, LANES)]

    where = (g, across, r, core, me, sib, n)
    ab = Gather(where, ab_region, ab_send, ab_recv)
    w = Gather(where, w_region, w_send, w_recv)

    loads[0].wait()
    loads[1].wait()
    ab.begin()
    loads[2].wait()
    w.begin()
    for s in range(n - 1):
        ab.step(s)
        if s == n // 2:
            w.step(0)
    for d in range(n):
        ab.whole(d)

    row = lax.broadcasted_iota(jnp.int32, (rows, picked), 0) // BLK
    col = lax.broadcasted_iota(jnp.int32, (rows, picked), 1) // rank
    mine = row == col
    tag = jnp.zeros((picked, LANES), jnp.float32)
    at = lax.broadcasted_iota(jnp.int32, (picked, LANES), 0) // rank
    b_parts = []
    for k in range(blocks):
        slot = slots[k]
        a_sel[k * rank : (k + 1) * rank, :] = abg[slot, :, 0:width]
        b_parts.append(abg[slot, :, width : width + kv])
        tag = jnp.where(at == k, slot.astype(jnp.float32), tag)
    tag = tag.astype(jnp.bfloat16)
    b_sel = jnp.concatenate(b_parts, axis=0)
    wide = low_rank_scale * lax.dot_general(go[...], b_sel, NT, preferred_element_type=jnp.float32)
    low[...] = jnp.where(mine, wide, 0.0).astype(jnp.bfloat16)
    loads[3].wait()

    def parts(p, inner):
        cols = pl.ds(pl.multiple_of(p * piece, piece), piece)
        x = feat[:, cols]
        part = lax.dot_general(low[...], x, TN, preferred_element_type=jnp.float32)
        sent[p, :, 0:piece] = part.astype(jnp.bfloat16)
        sent[p, :, piece + LANES : piece + 2 * LANES] = tag
        return inner + lax.dot_general(x, a_sel[:, cols], NT, preferred_element_type=jnp.float32)

    inner = lax.fori_loop(0, zero, parts, jnp.zeros((rows, picked), jnp.float32))
    w.step(1)
    inner = jnp.where(mine, inner, 0.0).astype(jnp.bfloat16)
    part_b = low_rank_scale * lax.dot_general(
        inner, go[...], TN, preferred_element_type=jnp.float32
    )
    part_b = part_b.astype(jnp.bfloat16)
    again = zero // (kv // LANES)
    for p in range(zero):
        c = p // again
        sent[p, :, piece : piece + LANES] = part_b[:, c * LANES : (c + 1) * LANES]

    def part_copy(i):
        to = (me + i) % zero
        return pltpu.make_async_remote_copy(
            src_ref=sent.at[to], dst_ref=got.at[me], send_sem=p_send.at[i],
            recv_sem=p_recv.at[i], device_id=(g, to), device_id_type=MESH,
        )

    def final_copy(i):
        to = (me + i) % zero
        return pltpu.make_async_remote_copy(
            src_ref=summed.at[to], dst_ref=final.at[me], send_sem=f_send.at[i],
            recv_sem=f_recv.at[i], device_id=(g, to), device_id_type=MESH,
        )

    def each(act):
        def go_on(i, c):
            act(i)
            return c

        lax.fori_loop(1, zero, go_on, 0)

    each(lambda i: part_copy(i).start())
    got[me] = sent[me]

    def base(d, order):
        def one(k, c):
            z = chip_at((r - d + n) % n, n) * 2 + k
            cols = pl.ds(pl.multiple_of(z * held, held), held)
            total = lax.dot_general(go[...], wg[z], NT, preferred_element_type=jnp.float32)
            total += jnp.dot(low[...], a_sel[:, cols], preferred_element_type=jnp.float32)
            out[:, cols] = total.astype(jnp.bfloat16)
            pltpu.make_async_copy(out.at[:, cols], gi.at[:, cols], stored.at[2 * order + k]).start()
            return c

        w.whole(d)
        lax.fori_loop(0, 2, one, 0)

    def add_up():
        each(lambda i: part_copy(i).wait_recv())
        total = zero * picked
        sources = got[...].reshape(total, piece + 2 * LANES)
        tags = sources[:, piece + LANES :].astype(jnp.float32)
        values = sources[:, : piece + LANES]
        r_at = lax.broadcasted_iota(jnp.int32, (total, LANES), 0) % rank
        l_at = lax.broadcasted_iota(jnp.int32, (total, LANES), 1)
        same = r_at == l_at % rank
        per = LANES // rank
        for e in range(tenants // per):
            targets = (l_at // rank + e * per).astype(jnp.float32)
            member = jnp.where(same & (tags == targets), 1.0, 0.0).astype(jnp.bfloat16)
            sums = lax.dot_general(member, values, TN, preferred_element_type=jnp.float32)
            count = lax.dot_general(
                member, jnp.ones((total, LANES), jnp.bfloat16), TN,
                preferred_element_type=jnp.float32,
            )
            sums = sums / (BLK * count[:, 0:1])
            summed[e * per : (e + 1) * per] = sums.reshape(per, rank, piece + LANES)
        each(lambda i: final_copy(i).start())
        final[me] = summed[me]

    base(0, 0)
    order, ready = 1, []
    for s in range(2, n - 1):
        w.step(s)
        if s == 3:
            add_up()
        for d in ready:
            base(d, order)
            order += 1
        ready = sorted({d for d in (s + 1, n - 1 - s) if 2 * s + 2 >= n})
    for d in ready:
        base(d, order)
        order += 1

    each(lambda i: final_copy(i).wait_recv())
    for p in range(zero):
        ga[:, p * piece : (p + 1) * piece] = final[p, :, 0:piece]
    for c in range(kv // LANES):
        gb[:, c * LANES : (c + 1) * LANES] = final[c * again, :, piece : piece + LANES]
    ab.end()
    w.end()
    each(lambda i: part_copy(i).wait_send())
    each(lambda i: final_copy(i).wait_send())

    def written(i, c):
        cols = pl.ds(pl.multiple_of(i * held, held), held)
        pltpu.make_async_copy(out.at[:, cols], gi.at[:, cols], stored.at[i]).wait()
        return c

    lax.fori_loop(0, zero, written, 0)


def body(features, grad_out, base_weight, factor_a, factor_b, tenant_ids, owner_of):
    zero = lax.axis_size("zero")
    rows, width = features.shape
    kv = grad_out.shape[1]
    rank = factor_a.shape[2]
    held = base_weight.shape[0]
    blocks = rows // BLK
    piece = width // zero
    picked = blocks * rank
    n = zero // 2
    slots = jnp.take(slot_table(owner_of), tenant_ids.reshape(blocks, BLK)[:, 0])
    bf16, f32 = jnp.bfloat16, jnp.float32
    vmem = pl.BlockSpec(memory_space=pltpu.VMEM)
    anywhere = pl.BlockSpec(memory_space=pl.ANY)
    dma = pltpu.SemaphoreType.DMA
    grad_in, grad_at, grad_b = pl.pallas_call(
        functools.partial(kernel, zero),
        out_shape=(
            jax.ShapeDtypeStruct((rows, width), bf16),
            jax.ShapeDtypeStruct((rank, width), f32),
            jax.ShapeDtypeStruct((rank, kv), f32),
        ),
        in_specs=[
            pl.BlockSpec(memory_space=pltpu.SMEM), anywhere, vmem, anywhere, anywhere, anywhere,
        ],
        out_specs=(anywhere, vmem, vmem),
        scratch_shapes=[
            pltpu.VMEM((rows, width), bf16),
            pltpu.VMEM((rows, width), bf16),
            pltpu.VMEM((zero, held, kv), bf16),
            pltpu.VMEM((zero, rank, width + kv), bf16),
            pltpu.VMEM((picked, width), bf16),
            pltpu.VMEM((rows, picked), bf16),
            pltpu.VMEM((zero, picked, piece + 2 * LANES), bf16),
            pltpu.VMEM((zero, picked, piece + 2 * LANES), bf16),
            pltpu.VMEM((zero, rank, piece + LANES), f32),
            pltpu.VMEM((zero, rank, piece + LANES), f32),
            dma((4,)),
            dma((zero,)),
            dma((7, n - 1)),
            dma((7, n - 1)),
            dma((7, n - 1)),
            dma((7, n - 1)),
            dma((zero,)),
            dma((zero,)),
            dma((zero,)),
            dma((zero,)),
        ],
        compiler_params=pltpu.CompilerParams(
            collective_id=0, has_side_effects=True, vmem_limit_bytes=58 * 2**20
        ),
        cost_estimate=pl.CostEstimate(
            flops=2 * rows * width * (kv + 3 * picked),
            bytes_accessed=2 * (2 * rows * width + width * kv),
            transcendentals=0,
        ),
    )(
        slots,
        features,
        grad_out,
        base_weight,
        jnp.swapaxes(factor_a[0], 0, 1),
        factor_b[0],
    )
    return grad_in, jnp.swapaxes(grad_at, 0, 1)[None], grad_b[None]


def solution(mesh):
    placed = (
        P(("groups", "zero"), None),
        P(("groups", "zero"), None),
        P("zero", None),
        P("zero", None, None),
        P("zero", None, None),
        P(("groups", "zero")),
        P(),
    )
    return jax.shard_map(
        body,
        mesh=mesh,
        in_specs=placed,
        out_specs=(
            P(("groups", "zero"), None),
            P(("groups", "zero"), None, None),
            P(("groups", "zero"), None, None),
        ),
        check_vma=False,
    )
```

time: 233 us -> 153 us (0.66)
  Pallas kernels: 0 us -> 141 us
  waiting for transfers between devices: 79.6 us -> 0 us
  starting transfers between devices: 47.1 us -> 0 us
  local copies, waits for them, and re-layouts: 41.3 us -> 6.77 us
  matrix products: 28.3 us -> 0 us
  between operations: 14.9 us -> 0.66 us
  blocking collectives: 12.5 us -> 0 us
  other arithmetic: 8.06 us -> 3.69 us
    pallas_call x0 -> x1, Pallas kernels: none -> 141 us  [body(): pl.pallas_call(functools.partial(kernel, zero), out_shape=(jax.ShapeDtype...]
    all_to_all x8 -> x0, waiting for transfers between devices: 78.9 us -> none  [the longest x1 28.3 us: body(): lax.all_to_all(part_a.reshape(block_count, width_zero, piece_a), 'zero',...]
    all_to_all x8 -> x0, starting transfers between devices: 47 us -> none  [the longest x1 10.3 us: body(): lax.all_to_all(part_b.reshape(block_count, width_zero, piece_b), 'zero',...]
    dot_general x7 -> x0, matrix products: 28.3 us -> none  [the longest x1 12.3 us: body(): lax.dot_general(grad_out, full_weight, (((1,), (1,)), ((), ())), preferre...]
    reshape x7 -> x0, local copies, waits for them, and re-layouts: 19.2 us -> none  [the longest x2 9.67 us: body(): part_a.reshape(block_count, width_zero, piece_a)]
    all_gather x1 -> x0, blocking collectives: 12.5 us -> none  [body(): every_id = lax.all_gather(block_ids, 'zero', axis=0, tiled=True)]
    unnamed x16 -> x7, local copies, waits for them, and re-layouts: 11 us -> 6.13 us
    dot_general x1 -> x0, local copies, waits for them, and re-layouts: 4.6 us -> none  [body(): jnp.einsum('nrd,nrj->ndj', blocked_in, low_proj, preferred_element_type=j...]
  transfers between devices with their start and end apart: 9 -> 0, of which waited for: 6 -> 0; matrix products, arithmetic and copies ran while one was open for 28% -> 0% of each run, Pallas kernels for 0% -> 0%
where the time goes in v1:
time: 153 us; the launch traced here: 152 us
  Pallas kernels  141 us (92%)
  local copies, waits for them, and re-layouts  6.77 us (4%)
  other arithmetic  3.69 us (2%)
    pallas_call x1, Pallas kernels, body(): pl.pallas_call(functools.partial(kernel, zero), out_shape=(jax.ShapeDtype...  141 us
    unnamed x7, local copies, waits for them, and re-layouts  6.13 us

profile of v1, /device:TPU:0, one launch (start us, length us, event | category | flops | bytes accessed | tf_op | source)
XLA Modules:
  0.0 152.3 jit_solution(14335662164334595742)
XLA Ops:
  0.6 0.8 and_reduce_fusion
  1.4 0.8 fusion.1
  2.2 0.9 convert_reduce_fusion
  3.1 0.7 add.10
  3.8 0.6 gather_fusion
  4.4 0.5 broadcast_select_fusion.slots
  5.0 141.2 %shard_map.94 = (bf16[256,8192]{1,0:T(8,128)(2,1)}, f32[16,8192]{1,0:T(8,128)}, f32[16,1024]{1,0:T(8,128)}) custom-call(s32[2]{0:T(128)} %broadcast_select_fusion.slots, bf16[256,8192]{1,0:T(8,128)(2,1)} %feat_in.1, bf16[256,1024]{1,0:T(8,128)(2,1)} %go.1, bf16[512,1024]{1,0:T(8,128)(2,1)} %w_in.1, bf16[16,8192]{1,0:T(8,128)(2,1)} %bitcast.11, ...), custom_call_target="tpu_custom_call" | custom-call | flops 4697620480 | bytes 25165824 | tf_op jit(solution)/shard_map/pallas_call | solution.py:345
  146.1 0.0 copy-start
  146.2 0.0 copy-start.1
  146.2 4.7 %copy.13 = bf16[256,8192]{1,0:T(8,128)(2,1)} copy(bf16[256,8192]{1,0:T(8,128)(2,1)} %get-tuple-element.12) | data formatting | bytes 8388608
  150.9 0.0 copy-done
  150.9 0.8 copy.14
  151.7 0.0 copy-done.1
  151.7 0.6 copy.15
  (1 shorter events, 0.0 us)
Async XLA Ops:
  146.1 4.7 %copy-start = (f32[16,8192]{1,0:T(8,128)S(1)}, f32[16,8192]{1,0:T(8,128)}, u32[]{:S(2)}) copy-start(f32[16,8192]{1,0:T(8,128)} %get-tuple-element.7) | copy-start | bytes 1572868
  146.2 5.5 %copy-start.1 = (f32[16,1024]{1,0:T(8,128)S(1)}, f32[16,1024]{1,0:T(8,128)}, u32[]{:S(2)}) copy-start(f32[16,1024]{1,0:T(8,128)} %get-tuple-element.8) | copy-start | bytes 196612

commit v2 on v1

--- a/solution.py
+++ b/solution.py
@@ -13,14 +13,17 @@
 MESH = pl.DeviceIdType.MESH
 NT = (((1,), (1,)), ((), ()))
 TN = (((0,), (0,)), ((), ()))
-CW, CCW, ACROSS, SIB_CW, SIB_CCW, SIB_ACROSS, SIB_OWN = range(7)
-
-
-def slot_table(owner_of):
-    tenant_count = owner_of.shape[0]
-    positions = jnp.arange(tenant_count, dtype=jnp.int32)
-    before = (owner_of[None, :] == owner_of[:, None]) & (positions[None, :] < positions[:, None])
-    return owner_of + jnp.sum(before.astype(jnp.int32), axis=1)
+PLAN = {"cuts": 4, "after": (2, 2, 2, 2), "add": 4}
+CW, CCW, ACROSS_CW, ACROSS_CCW, SIB_CW, SIB_CCW, SIB_ACROSS_CW, SIB_ACROSS_CCW, OWN = range(9)
+
+
+def slot_of(tenant, owner_of):
+    owner = owner_of[tenant]
+
+    def count(u, slot):
+        return slot + jnp.where((owner_of[u] == owner) & (u < tenant), 1, 0)
+
+    return lax.fori_loop(0, owner_of.shape[0], count, owner)
 
 
 def chip_at(pos, chips):
@@ -39,31 +42,29 @@
 class Gather:
     def __init__(self, where, region, send, recv):
         self.where, self.region, self.send, self.recv = where, region, send, recv
+        self.half = where[-1] // 2
         self.started, self.received = [], set()
 
     def copy(self, kind, s):
         g, across, r, core, me, sib, n = self.where
-        if kind == SIB_OWN:
-            pos, part = r, None
-        elif kind == CW:
-            pos, part = r - s + n, 0
-        elif kind == CCW:
-            pos, part = r + s, 1
-        elif kind in (ACROSS, SIB_CW):
-            pos, part = r - 1 - s + n, 0
-        elif kind == SIB_CCW:
-            pos, part = r + 1 + s, 1
+        ahead = 1 - 2 * core
+        way = -ahead if kind in (CW, ACROSS_CW, SIB_CW, SIB_ACROSS_CW) else ahead
+        back = kind in (CCW, SIB_CCW)
+        if kind == OWN:
+            pos, part, to = r, None, (g, sib)
+        elif kind in (CW, CCW):
+            pos = r + s * way
+            to = (g, chip_at((r - way + n) % n, n) * 2 + core)
         else:
-            pos, part = r - 1 - s + n, 2
-        if kind == CW:
-            to = (g, chip_at((r + 1) % n, n) * 2 + core)
-        elif kind == CCW:
-            to = (g, chip_at((r + n - 1) % n, n) * 2 + core)
-        elif kind == ACROSS:
-            to = (across, me)
-        else:
-            to = (g, sib)
-        ref = self.region(chip_at(pos % n, n) * 2 + core, part)
+            pos = r + (1 + s) * way
+            to = (across, me) if kind in (ACROSS_CW, ACROSS_CCW) else (g, sib)
+        if kind in (CW, CCW, SIB_CW, SIB_CCW):
+            part = (1 if back else 0) if s == self.half - 1 else 3
+        elif kind in (ACROSS_CW, ACROSS_CCW):
+            part = 0
+        elif kind != OWN:
+            part = 2
+        ref = self.region(chip_at((pos + n) % n, n) * 2 + core, part)
         return pltpu.make_async_remote_copy(
             src_ref=ref,
             dst_ref=ref,
@@ -85,38 +86,39 @@
     def begin(self):
         self.start(CW, 0)
         self.start(CCW, 0)
-        self.start(SIB_OWN, 0)
+        self.start(OWN, 0)
 
     def step(self, s):
-        n = self.where[-1]
-        self.need(CW, s)
-        if s < n - 2:
-            self.start(CW, s + 1)
-        self.start(ACROSS, s)
-        self.start(SIB_CW, s)
-        self.need(CCW, s)
-        if s < n - 2:
-            self.start(CCW, s + 1)
-        self.start(SIB_CCW, s)
+        last = s == self.half - 1
+        for kind in (CW, CCW):
+            self.need(kind, s)
+            if not last:
+                self.start(kind, s + 1)
+            if kind == CW or not last:
+                self.start(ACROSS_CW + kind, s)
+            self.start(SIB_CW + kind, s)
         if s >= 1:
-            self.need(ACROSS, s - 1)
-            self.start(SIB_ACROSS, s - 1)
-        if s == n - 2:
-            self.need(ACROSS, s)
-            self.start(SIB_ACROSS, s)
+            self.pass_on(s - 1, (CW, CCW))
+        if last:
+            self.pass_on(s, (CW,))
+
+    def pass_on(self, s, kinds):
+        for kind in kinds:
+            self.need(ACROSS_CW + kind, s)
+            self.start(SIB_ACROSS_CW + kind, s)
 
     def whole(self, d):
-        n = self.where[-1]
+        half, n = self.half, self.where[-1]
         if d == 0:
-            self.need(SIB_OWN, 0)
+            needs = [(OWN, 0)]
+        elif d == half:
+            needs = [(k, half - 1) for k in (CW, CCW, ACROSS_CW, SIB_CW, SIB_CCW, SIB_ACROSS_CW)]
+        elif d < half:
+            needs = [(k, d - 1) for k in (CW, ACROSS_CW, SIB_CCW, SIB_ACROSS_CCW)]
         else:
-            for own, other, s in (
-                (CW, SIB_CW, d - 1),
-                (CCW, SIB_CCW, n - 1 - d),
-                (ACROSS, SIB_ACROSS, d - 1),
-            ):
-                self.need(own, s)
-                self.need(other, s)
+            needs = [(k, n - d - 1) for k in (CCW, ACROSS_CCW, SIB_CW, SIB_ACROSS_CW)]
+        for need in needs:
+            self.need(*need)
 
     def end(self):
         for kind, s in self.started:
@@ -124,7 +126,7 @@
 
 
 def kernel(
-    zero, slots, feat_in, go, w_in, at_in, b_in, gi, ga, gb,
+    zero, plan, tenant_ids, owner_of, feat_in, go, w_in, at_in, b_in, gi, ga, gb,
     feat, out, wg, abg, a_sel, low, sent, got, summed, final,
     load, stored, w_send, w_recv, ab_send, ab_recv, p_send, p_recv, f_send, f_recv,
 ):
@@ -165,17 +167,24 @@
     lax.fori_loop(1, zero, greet, 0)
     pl.semaphore_wait(barrier, zero)
 
-    w_third = -(-held // 48) * 16
-    ab_third = -(-(width + kv) // (3 * LANES)) * LANES
+    cuts = plan["cuts"]
+    sub = held // cuts
+    w_third = -(-sub * 3 // 128) * 16
+    ab_third = (width + kv) * 3 // (8 * LANES) * LANES
 
     def cut(total, third, part, unit):
         if part == 1:
             return pl.ds(third, total - 2 * third)
+        if part == 3:
+            return pl.ds(pl.multiple_of(parity * third, unit), total - third)
         at = (parity if part == 0 else 1 - parity) * (total - third)
         return pl.ds(pl.multiple_of(at, unit), third)
 
-    def w_region(i, part):
-        return wg.at[i] if part is None else wg.at[i, cut(held, w_third, part, 16), :]
+    def w_region(e, i, part):
+        if part is None:
+            return wg.at[i, pl.ds(e * sub, sub), :]
+        rows_of = cut(sub, w_third, part, 16)
+        return wg.at[i, pl.ds(pl.multiple_of(e * sub + rows_of.start, 16), rows_of.size), :]
 
     def ab_region(i, part):
         if part is None:
@@ -184,19 +193,30 @@
 
     where = (g, across, r, core, me, sib, n)
     ab = Gather(where, ab_region, ab_send, ab_recv)
-    w = Gather(where, w_region, w_send, w_recv)
+    ws = [
+        Gather(where, functools.partial(w_region, e), w_send.at[e], w_recv.at[e])
+        for e in range(cuts)
+    ]
 
     loads[0].wait()
     loads[1].wait()
     ab.begin()
     loads[2].wait()
-    w.begin()
-    for s in range(n - 1):
+    for w in ws:
+        w.begin()
+    turns = [(s, e) for s in range(n // 2) for e in range(cuts)]
+    after = plan["after"]
+    for s in range(n // 2):
         ab.step(s)
-        if s == n // 2:
-            w.step(0)
+        for _ in range(after[s] if s < len(after) else 0):
+            t, e = turns.pop(0)
+            ws[e].step(t)
     for d in range(n):
         ab.whole(d)
+
+    def advance():
+        s, e = turns.pop(0)
+        ws[e].step(s)
 
     row = lax.broadcasted_iota(jnp.int32, (rows, picked), 0) // BLK
     col = lax.broadcasted_iota(jnp.int32, (rows, picked), 1) // rank
@@ -205,11 +225,10 @@
     at = lax.broadcasted_iota(jnp.int32, (picked, LANES), 0) // rank
     b_parts = []
     for k in range(blocks):
-        slot = slots[k]
+        slot = slot_of(tenant_ids[k * BLK], owner_of)
         a_sel[k * rank : (k + 1) * rank, :] = abg[slot, :, 0:width]
         b_parts.append(abg[slot, :, width : width + kv])
         tag = jnp.where(at == k, slot.astype(jnp.float32), tag)
-    tag = tag.astype(jnp.bfloat16)
     b_sel = jnp.concatenate(b_parts, axis=0)
     wide = low_rank_scale * lax.dot_general(go[...], b_sel, NT, preferred_element_type=jnp.float32)
     low[...] = jnp.where(mine, wide, 0.0).astype(jnp.bfloat16)
@@ -220,20 +239,20 @@
         x = feat[:, cols]
         part = lax.dot_general(low[...], x, TN, preferred_element_type=jnp.float32)
         sent[p, :, 0:piece] = part.astype(jnp.bfloat16)
-        sent[p, :, piece + LANES : piece + 2 * LANES] = tag
         return inner + lax.dot_general(x, a_sel[:, cols], NT, preferred_element_type=jnp.float32)
 
     inner = lax.fori_loop(0, zero, parts, jnp.zeros((rows, picked), jnp.float32))
-    w.step(1)
+    advance()
     inner = jnp.where(mine, inner, 0.0).astype(jnp.bfloat16)
     part_b = low_rank_scale * lax.dot_general(
         inner, go[...], TN, preferred_element_type=jnp.float32
     )
-    part_b = part_b.astype(jnp.bfloat16)
     again = zero // (kv // LANES)
+    lane = lax.broadcasted_iota(jnp.int32, (picked, LANES), 1) * again // LANES
     for p in range(zero):
         c = p // again
-        sent[p, :, piece : piece + LANES] = part_b[:, c * LANES : (c + 1) * LANES]
+        chunk = jnp.where(lane == p % again, part_b[:, c * LANES : (c + 1) * LANES], tag)
+        sent[p, :, piece : piece + LANES] = chunk.astype(jnp.bfloat16)
 
     def part_copy(i):
         to = (me + i) % zero
@@ -259,9 +278,11 @@
     each(lambda i: part_copy(i).start())
     got[me] = sent[me]
 
+    made = []
+
     def base(d, order):
         def one(k, c):
-            z = chip_at((r - d + n) % n, n) * 2 + k
+            z = chip_at((r - d * (1 - 2 * core) + n) % n, n) * 2 + k
             cols = pl.ds(pl.multiple_of(z * held, held), held)
             total = lax.dot_general(go[...], wg[z], NT, preferred_element_type=jnp.float32)
             total += jnp.dot(low[...], a_sel[:, cols], preferred_element_type=jnp.float32)
@@ -269,15 +290,18 @@
             pltpu.make_async_copy(out.at[:, cols], gi.at[:, cols], stored.at[2 * order + k]).start()
             return c
 
-        w.whole(d)
+        made.append(d)
+        for w in ws:
+            w.whole(d)
         lax.fori_loop(0, 2, one, 0)
 
     def add_up():
         each(lambda i: part_copy(i).wait_recv())
         total = zero * picked
-        sources = got[...].reshape(total, piece + 2 * LANES)
-        tags = sources[:, piece + LANES :].astype(jnp.float32)
-        values = sources[:, : piece + LANES]
+        values = got[...].reshape(total, piece + LANES)
+        lanes = lax.broadcasted_iota(jnp.int32, (total, LANES), 1) * again // LANES
+        tags = jnp.where(lanes == me % again, 0.0, values[:, piece:].astype(jnp.float32))
+        tags = jnp.max(tags, axis=1, keepdims=True)
         r_at = lax.broadcasted_iota(jnp.int32, (total, LANES), 0) % rank
         l_at = lax.broadcasted_iota(jnp.int32, (total, LANES), 1)
         same = r_at == l_at % rank
@@ -291,31 +315,40 @@
                 preferred_element_type=jnp.float32,
             )
             sums = sums / (BLK * count[:, 0:1])
-            summed[e * per : (e + 1) * per] = sums.reshape(per, rank, piece + LANES)
+            summed[e * per : (e + 1) * per] = sums.astype(jnp.bfloat16).reshape(per, rank, piece + LANES)
         each(lambda i: final_copy(i).start())
         final[me] = summed[me]
 
     base(0, 0)
-    order, ready = 1, []
-    for s in range(2, n - 1):
-        w.step(s)
-        if s == 3:
+    ready, taken = [], 0
+    while turns:
+        s, e = turns[0]
+        advance()
+        taken += 1
+        if taken == plan["add"]:
             add_up()
-        for d in ready:
-            base(d, order)
-            order += 1
-        ready = sorted({d for d in (s + 1, n - 1 - s) if 2 * s + 2 >= n})
-    for d in ready:
-        base(d, order)
-        order += 1
+        if e == cuts - 1:
+            for d in ready:
+                base(d, len(made))
+            ready = [d for d in (s + 1, n - 1 - s) if d not in made and s + 1 < n // 2]
+    if taken < plan["add"]:
+        add_up()
+    for d in range(n):
+        if d not in made:
+            base(d, len(made))
 
     each(lambda i: final_copy(i).wait_recv())
     for p in range(zero):
-        ga[:, p * piece : (p + 1) * piece] = final[p, :, 0:piece]
+        ga[:, p * piece : (p + 1) * piece] = final[p, :, 0:piece].astype(jnp.float32)
     for c in range(kv // LANES):
-        gb[:, c * LANES : (c + 1) * LANES] = final[c * again, :, piece : piece + LANES]
+        total = jnp.zeros((rank, LANES), jnp.float32)
+        for e in range(again):
+            chunk = final[c * again + e, :, piece : piece + LANES].astype(jnp.float32)
+            total = jnp.where(lane[:rank] == e, chunk, total)
+        gb[:, c * LANES : (c + 1) * LANES] = total
     ab.end()
-    w.end()
+    for w in ws:
+        w.end()
     each(lambda i: part_copy(i).wait_send())
     each(lambda i: final_copy(i).wait_send())
 
@@ -337,20 +370,20 @@
     piece = width // zero
     picked = blocks * rank
     n = zero // 2
-    slots = jnp.take(slot_table(owner_of), tenant_ids.reshape(blocks, BLK)[:, 0])
     bf16, f32 = jnp.bfloat16, jnp.float32
     vmem = pl.BlockSpec(memory_space=pltpu.VMEM)
+    smem = pl.BlockSpec(memory_space=pltpu.SMEM)
     anywhere = pl.BlockSpec(memory_space=pl.ANY)
     dma = pltpu.SemaphoreType.DMA
     grad_in, grad_at, grad_b = pl.pallas_call(
-        functools.partial(kernel, zero),
+        functools.partial(kernel, zero, PLAN),
         out_shape=(
             jax.ShapeDtypeStruct((rows, width), bf16),
             jax.ShapeDtypeStruct((rank, width), f32),
             jax.ShapeDtypeStruct((rank, kv), f32),
         ),
         in_specs=[
-            pl.BlockSpec(memory_space=pltpu.SMEM), anywhere, vmem, anywhere, anywhere, anywhere,
+            smem, smem, anywhere, vmem, anywhere, anywhere, anywhere,
         ],
         out_specs=(anywhere, vmem, vmem),
         scratch_shapes=[
@@ -360,16 +393,16 @@
             pltpu.VMEM((zero, rank, width + kv), bf16),
             pltpu.VMEM((picked, width), bf16),
             pltpu.VMEM((rows, picked), bf16),
-            pltpu.VMEM((zero, picked, piece + 2 * LANES), bf16),
-            pltpu.VMEM((zero, picked, piece + 2 * LANES), bf16),
-            pltpu.VMEM((zero, rank, piece + LANES), f32),
-            pltpu.VMEM((zero, rank, piece + LANES), f32),
+            pltpu.VMEM((zero, picked, piece + LANES), bf16),
+            pltpu.VMEM((zero, picked, piece + LANES), bf16),
+            pltpu.VMEM((zero, rank, piece + LANES), bf16),
+            pltpu.VMEM((zero, rank, piece + LANES), bf16),
             dma((4,)),
             dma((zero,)),
-            dma((7, n - 1)),
-            dma((7, n - 1)),
-            dma((7, n - 1)),
-            dma((7, n - 1)),
+            dma((PLAN["cuts"], 9, n // 2)),
+            dma((PLAN["cuts"], 9, n // 2)),
+            dma((9, n // 2)),
+            dma((9, n // 2)),
             dma((zero,)),
             dma((zero,)),
             dma((zero,)),
@@ -384,7 +417,8 @@
             transcendentals=0,
         ),
     )(
-        slots,
+        tenant_ids,
+        owner_of,
         features,
         grad_out,
         base_weight,

time: 153 us -> 121 us (0.79)
  Pallas kernels: 141 us -> 114 us
  other arithmetic: 3.69 us -> 0 us
    pallas_call x1, Pallas kernels: 141 us -> 114 us  [body(): pl.pallas_call(functools.partial(kernel, zero, PLAN), out_shape=(jax.Shap...]
where the time goes in v2:
time: 121 us
  Pallas kernels  114 us (94%)
  local copies, waits for them, and re-layouts  6.13 us (5%)
    pallas_call x1, Pallas kernels, body(): pl.pallas_call(functools.partial(kernel, zero, PLAN), out_shape=(jax.Shap...  114 us
    unnamed x7, local copies, waits for them, and re-layouts  6.13 us

profile of v2, /device:TPU:0, one launch (start us, length us, event | category | flops | bytes accessed | tf_op | source)
XLA Modules:
  0.0 121.0 jit_solution(2142842134483893665)
XLA Ops:
  0.6 114.2 %shard_map.94 = (bf16[256,8192]{1,0:T(8,128)(2,1)}, f32[16,8192]{1,0:T(8,128)}, f32[16,1024]{1,0:T(8,128)}) custom-call(s32[256]{0:T(256)} %tenant_ids.1, s32[16]{0:T(128)} %owner_of.1, bf16[256,8192]{1,0:T(8,128)(2,1)} %feat_in.1, bf16[256,1024]{1,0:T(8,128)(2,1)} %go.1, bf16[512,1024]{1,0:T(8,128)(2,1)} %w_in.1, bf16[16,8192]{1,0:T(8,128)(2,1)} %bitcast.10, ...), custom_call_target="tpu_custom_call" | custom-call | flops 4697620480 | bytes 25165824 | tf_op jit(solution)/shard_map/pallas_call | solution.py:378
  114.9 0.0 copy-start
  114.9 0.0 copy-start.1
  114.9 4.7 %copy.13 = bf16[256,8192]{1,0:T(8,128)(2,1)} copy(bf16[256,8192]{1,0:T(8,128)(2,1)} %get-tuple-element.12) | data formatting | bytes 8388608
  119.6 0.0 copy-done
  119.6 0.8 copy.14
  120.4 0.0 copy-done.1
  120.4 0.6 copy.15
Async XLA Ops:
  114.9 4.7 %copy-start = (f32[16,8192]{1,0:T(8,128)S(1)}, f32[16,8192]{1,0:T(8,128)}, u32[]{:S(2)}) copy-start(f32[16,8192]{1,0:T(8,128)} %get-tuple-element.7) | copy-start | bytes 1572868
  114.9 5.5 %copy-start.1 = (f32[16,1024]{1,0:T(8,128)S(1)}, f32[16,1024]{1,0:T(8,128)}, u32[]{:S(2)}) copy-start(f32[16,1024]{1,0:T(8,128)} %get-tuple-element.8) | copy-start | bytes 196612

commit v3 on v2

--- a/solution.py
+++ b/solution.py
@@ -13,7 +13,7 @@
 MESH = pl.DeviceIdType.MESH
 NT = (((1,), (1,)), ((), ()))
 TN = (((0,), (0,)), ((), ()))
-PLAN = {"cuts": 4, "after": (2, 2, 2, 2), "add": 4}
+PLAN = {"cuts": 4, "w": (3, 3, 3, 2), "ab": 21, "after": (2, 2, 2, 2), "add": 4}
 CW, CCW, ACROSS_CW, ACROSS_CCW, SIB_CW, SIB_CCW, SIB_ACROSS_CW, SIB_ACROSS_CCW, OWN = range(9)
 
 
@@ -167,10 +167,10 @@
     lax.fori_loop(1, zero, greet, 0)
     pl.semaphore_wait(barrier, zero)
 
-    cuts = plan["cuts"]
+    cuts = min(plan["cuts"], held // 64)
     sub = held // cuts
-    w_third = -(-sub * 3 // 128) * 16
-    ab_third = (width + kv) * 3 // (8 * LANES) * LANES
+    w_thirds = [sub * eighths // 128 * 16 for eighths in plan["w"]]
+    ab_third = (width + kv) * plan["ab"] // (72 * LANES) * LANES
 
     def cut(total, third, part, unit):
         if part == 1:
@@ -183,7 +183,7 @@
     def w_region(e, i, part):
         if part is None:
             return wg.at[i, pl.ds(e * sub, sub), :]
-        rows_of = cut(sub, w_third, part, 16)
+        rows_of = cut(sub, w_thirds[e], part, 16)
         return wg.at[i, pl.ds(pl.multiple_of(e * sub + rows_of.start, 16), rows_of.size), :]
 
     def ab_region(i, part):

time: 121 us -> 117 us (0.967)
  Pallas kernels: 114 us -> 110 us
    pallas_call x1, Pallas kernels: 114 us -> 110 us  [body(): pl.pallas_call(functools.partial(kernel, zero, PLAN), out_shape=(jax.Shap...]
where the time goes in v3:
time: 117 us
  Pallas kernels  110 us (94%)
  local copies, waits for them, and re-layouts  6.13 us (5%)
    pallas_call x1, Pallas kernels, body(): pl.pallas_call(functools.partial(kernel, zero, PLAN), out_shape=(jax.Shap...  110 us
    unnamed x7, local copies, waits for them, and re-layouts  6.13 us

profile of v3, /device:TPU:0, one launch (start us, length us, event | category | flops | bytes accessed | tf_op | source)
XLA Modules:
  0.0 116.5 jit_solution(7394025245839784722)
XLA Ops:
  0.6 109.7 %shard_map.94 = (bf16[256,8192]{1,0:T(8,128)(2,1)}, f32[16,8192]{1,0:T(8,128)}, f32[16,1024]{1,0:T(8,128)}) custom-call(s32[256]{0:T(256)} %tenant_ids.1, s32[16]{0:T(128)} %owner_of.1, bf16[256,8192]{1,0:T(8,128)(2,1)} %feat_in.1, bf16[256,1024]{1,0:T(8,128)(2,1)} %go.1, bf16[512,1024]{1,0:T(8,128)(2,1)} %w_in.1, bf16[16,8192]{1,0:T(8,128)(2,1)} %bitcast.10, ...), custom_call_target="tpu_custom_call" | custom-call | flops 4697620480 | bytes 25165824 | tf_op jit(solution)/shard_map/pallas_call | solution.py:378
  110.4 0.0 copy-start
  110.4 0.0 copy-start.1
  110.4 4.7 %copy.13 = bf16[256,8192]{1,0:T(8,128)(2,1)} copy(bf16[256,8192]{1,0:T(8,128)(2,1)} %get-tuple-element.12) | data formatting | bytes 8388608
  115.1 0.0 copy-done
  115.1 0.8 copy.14
  115.9 0.0 copy-done.1
  115.9 0.6 copy.15
Async XLA Ops:
  110.4 4.7 %copy-start = (f32[16,8192]{1,0:T(8,128)S(1)}, f32[16,8192]{1,0:T(8,128)}, u32[]{:S(2)}) copy-start(f32[16,8192]{1,0:T(8,128)} %get-tuple-element.7) | copy-start | bytes 1572868
  110.4 5.5 %copy-start.1 = (f32[16,1024]{1,0:T(8,128)S(1)}, f32[16,1024]{1,0:T(8,128)}, u32[]{:S(2)}) copy-start(f32[16,1024]{1,0:T(8,128)} %get-tuple-element.8) | copy-start | bytes 196612
